TPU v7x, 256 devices: a whole 4x4x8 slice. The times are simulated.
256 devices in a mesh: seq: 64 (over z, y, x_lo), ch: 4 (over x_hi, core).
Axes of the slice: x: 4 (x_hi: 2, x_lo: 2; x = x_hi * 2 + x_lo), y: 4, z: 8, core: 2. Of those that a mesh axis runs over, the one named last changes fastest.
Arguments:
- tokens: bfloat16 [16384, 4096], P('seq', 'ch'), may hold values from -6 to 6
- in_weight: bfloat16 [4096, 3, 2048], P('seq', None, 'ch'), may hold values from -0.09375 to 0.09375
- short_filter: float32 [3, 3, 2048], P(None, None, 'ch'), may hold values from -3 to 3
- long_filter: float32 [16384, 2048], P('seq', 'ch'), may hold values from -0.046875 to 0.046875
- skip_gain: float32 [2048], P('ch'), may hold values from -4 to 4
Outputs:
- mixed: bfloat16 [16384, 2048], P('seq', 'ch')
All inputs are finite; a program needn't handle non-finite values.
Results may differ from a plain program's by a relative error of at most 0.0019.
Values may be sent and summed in bfloat16 or wider, within the bound.
A program may use at most 128 MiB of HBM per device.

v0:
```python
import math

import jax
import jax.numpy as jnp
from jax import lax
from jax.sharding import PartitionSpec as P

SHORT = 3


def shifted(shard, axis, by):
    peers = lax.axis_size(axis)
    pairs = [(i, i + by) for i in range(peers) if 0 <= i + by < peers]
    return lax.ppermute(shard, axis, pairs)


def dft_tables(row_count, col_count, modulus):
    row_index = lax.broadcasted_iota(jnp.int32, (row_count, col_count), 0)
    col_index = lax.broadcasted_iota(jnp.int32, (row_count, col_count), 1)
    phases = (row_index * col_index % modulus).astype(jnp.float32) * (2.0 * math.pi / modulus)
    return (jnp.cos(phases), jnp.sin(phases))


def left_apply(matrix, values):
    return jnp.dot(
        matrix, values, precision=lax.Precision.HIGHEST, preferred_element_type=jnp.float32
    )


def along_time(matrix, values):
    return jnp.einsum(
        "uv,jvc->juc",
        matrix,
        values,
        precision=lax.Precision.HIGHEST,
        preferred_element_type=jnp.float32,
    )


def local(tokens, in_weight, short_filter, long_filter, skip_gain):
    shards = lax.axis_size("seq")
    seq_rank = lax.axis_index("seq")
    tok_rows = tokens.shape[0]
    ch_width = skip_gain.shape[0]
    sub_rows = tok_rows // shards
    total_len = 2 * shards * tok_rows
    inverse_scale = 1.0 / total_len
    halo_rows = SHORT - 1
    features = lax.all_gather(tokens, "ch", axis=1, tiled=True)
    weight_piece = lax.all_gather(in_weight, "seq", axis=0, tiled=True)
    piece_rows = weight_piece.shape[0]
    flat_piece = weight_piece.reshape(piece_rows, 3 * ch_width)
    projected = jnp.dot(features, flat_piece, preferred_element_type=jnp.float32)
    previous_rows = shifted(projected[tok_rows - halo_rows :], "seq", 1)
    extended = jnp.concatenate([previous_rows, projected], axis=0)
    short_taps = short_filter.reshape(SHORT, 3 * ch_width)
    short_conv = jnp.zeros((tok_rows, 3 * ch_width), jnp.float32)
    for offset in range(SHORT):
        start_row = halo_rows - offset
        short_conv = short_conv + short_taps[offset] * extended[start_row : start_row + tok_rows]
    outer_gate = short_conv[:, :ch_width]
    gate_product = short_conv[:, ch_width : 2 * ch_width] * short_conv[:, 2 * ch_width :]
    cos_time, sin_time = dft_tables(tok_rows, tok_rows, tok_rows)
    paired = jnp.concatenate([gate_product, long_filter], axis=1)
    pair_width = 2 * ch_width
    outgoing = jnp.stack([paired, jnp.zeros_like(paired)]).reshape(2, shards, sub_rows, pair_width)
    cos_fwd, sin_fwd = dft_tables(2 * shards, 2 * shards, 2 * shards)
    received = lax.all_to_all(outgoing, "seq", split_axis=1, concat_axis=1, tiled=True)
    flat_cols = received.reshape(-1, sub_rows * pair_width)
    col_real = left_apply(cos_fwd, flat_cols).reshape(2 * shards, sub_rows, pair_width)
    col_imag = (-left_apply(sin_fwd, flat_cols)).reshape(2 * shards, sub_rows, pair_width)
    class_index = lax.broadcasted_iota(jnp.int32, (2 * shards, sub_rows), 0)
    time_index = seq_rank * sub_rows + lax.broadcasted_iota(jnp.int32, (2 * shards, sub_rows), 1)
    twist = (class_index * time_index % total_len).astype(jnp.float32) * (2.0 * math.pi / total_len)
    twist_cos = jnp.cos(twist)[:, :, None]
    twist_sin = jnp.sin(twist)[:, :, None]
    turned_real = col_real * twist_cos + col_imag * twist_sin
    turned_imag = col_imag * twist_cos - col_real * twist_sin
    freq_real, freq_imag = (
        lax.all_to_all(turned_real, "seq", split_axis=0, concat_axis=1, tiled=True),
        lax.all_to_all(turned_imag, "seq", split_axis=0, concat_axis=1, tiled=True),
    )
    spec_real = along_time(cos_time, freq_real) + along_time(sin_time, freq_imag)
    spec_imag = along_time(cos_time, freq_imag) - along_time(sin_time, freq_real)
    gate_real = spec_real[:, :, :ch_width]
    gate_imag = spec_imag[:, :, :ch_width]
    kernel_real = spec_real[:, :, ch_width:]
    kernel_imag = spec_imag[:, :, ch_width:]
    prod_real = gate_real * kernel_real - gate_imag * kernel_imag
    prod_imag = gate_real * kernel_imag + gate_imag * kernel_real
    inv_real = along_time(cos_time, prod_real) - along_time(sin_time, prod_imag)
    inv_imag = along_time(cos_time, prod_imag) + along_time(sin_time, prod_real)
    local_class = 2 * seq_rank + lax.broadcasted_iota(jnp.int32, (2, tok_rows), 0)
    local_time = lax.broadcasted_iota(jnp.int32, (2, tok_rows), 1)
    back_twist = (local_class * local_time % total_len).astype(jnp.float32) * (
        2.0 * math.pi / total_len
    )
    back_cos = jnp.cos(back_twist)[:, :, None]
    back_sin = jnp.sin(back_twist)[:, :, None]
    back_real = inv_real * back_cos - inv_imag * back_sin
    back_imag = inv_imag * back_cos + inv_real * back_sin
    cols_real, cols_imag = (
        lax.all_to_all(back_real, "seq", split_axis=1, concat_axis=0, tiled=True),
        lax.all_to_all(back_imag, "seq", split_axis=1, concat_axis=0, tiled=True),
    )
    cols_real = cols_real.reshape(2 * shards, sub_rows * ch_width)
    cols_imag = cols_imag.reshape(2 * shards, sub_rows * ch_width)
    cos_inv, sin_inv = dft_tables(2 * shards, 2 * shards, 2 * shards)
    positions = (left_apply(cos_inv, cols_real) - left_apply(sin_inv, cols_imag)) * inverse_scale
    leaving = positions.reshape(2, shards, sub_rows, ch_width)
    arrived = lax.all_to_all(leaving, "seq", split_axis=1, concat_axis=2, tiled=True)
    convolved = arrived[0, 0]
    return (outer_gate * (convolved + skip_gain * gate_product)).astype(jnp.bfloat16)


def solution(mesh):
    placed = (P("seq", "ch"), P("seq", None, "ch"), P(None, None, "ch"), P("seq", "ch"), P("ch"))
    return jax.shard_map(
        local, mesh=mesh, in_specs=placed, out_specs=P("seq", "ch"), check_vma=False
    )
```

profile of v0, /device:TPU:2, one launch (start us, length us, event | category | flops | bytes accessed | tf_op | source)
XLA Modules:
  0.0 723.8 jit_solution(429827828205433921)
XLA Ops:
  6.5 0.7 all-gather.5.cloned.1.call-update
  7.3 0.0 all-gather.3.cloned.1.call-start
  7.3 0.7 all-gather.3.cloned.1.call-update
  8.0 327.8 %all-gather.5.cloned.1.call-done = bf16[4096,3,512]{2,0,1:T(8,128)(2,1)} async-done(((bf16[64,3,512]{2,0,1:T(8,128)(2,1)}), bf16[4096,3,512]{2,0,1:T(8,128)(2,1)}) %all-gather.5.cloned.1.call-update) | async-done | bytes 12582928 | tf_op jit(solution)/shard_map/all_gather | solution.py:50
  335.8 17.1 %copy.42 = bf16[4096,3,512]{0,2,1:T(8,128)(2,1)} copy(bf16[4096,3,512]{2,0,1:T(8,128)(2,1)} %all-gather.5.cloned.1.call-done) | data formatting | bytes 25165824 | tf_op jit(solution)/shard_map/all_gather | solution.py:50
  353.0 12.8 %all-gather.3.cloned.1.call-done = bf16[256,4096]{1,0:T(8,128)(2,1)} async-done(((bf16[256,1024]{1,0:T(8,128)(2,1)}), bf16[256,4096]{1,0:T(8,128)(2,1)}) %all-gather.3.cloned.1.call-update) | async-done | bytes 2097168 | tf_op jit(solution)/shard_map/all_gather | solution.py:49
  365.8 7.1 fusion.111
  372.9 4.3 collective-permute-start
  377.3 0.0 copy-start.4
  377.3 1.3 collective-permute-done
  378.6 0.5 fusion.4
  379.1 1.1 copy-done.1
  380.2 0.1 slice_multiply_fusion
  380.3 0.1 maximum_bitcast_fusion
  380.4 0.2 stack.7
  380.7 1.7 reshape.126
  382.3 3.1 copy.43
  385.5 13.8 %all-to-all-start = ((f32[2,64,4,1024]{3,2,0,1:T(4,128)}), f32[2,64,4,1024]{3,2,0,1:T(4,128)S(1)}, u32[]{:S(2)}, u32[]{:S(2)}) async-start(f32[2,64,4,1024]{3,2,0,1:T(4,128)} %copy.43), calls=%async_computation | async-start | bytes 4194304 | tf_op jit(solution)/shard_map/all_to_all | solution.py:68
  399.3 0.1 fusion.59
  399.4 49.4 %all-to-all-done = f32[2,64,4,1024]{3,2,0,1:T(4,128)S(1)} async-done(((f32[2,64,4,1024]{3,2,0,1:T(4,128)}), f32[2,64,4,1024]{3,2,0,1:T(4,128)S(1)}, u32[]{:S(2)}, u32[]{:S(2)}) %all-to-all-start) | async-done | bytes 2097184 | tf_op jit(solution)/shard_map/all_to_all | solution.py:68
  448.8 0.2 copy.44
  448.9 1.6 copy.62
  450.6 3.4 convolution_negate_fusion
  454.0 2.9 copy.46
  456.9 2.9 copy.47
  459.8 1.8 copy.45
  461.6 6.0 multiply_add_fusion
  467.7 2.7 copy.48
  470.4 6.8 all-to-all-start.1
  477.2 4.3 copy.52
  481.5 45.0 %all-to-all-done.1 = f32[128,4,1024]{2,1,0:T(4,128)S(1)} async-done(((f32[128,4,1024]{2,1,0:T(4,128)}), f32[128,4,1024]{2,1,0:T(4,128)S(1)}, u32[]{:S(2)}, u32[]{:S(2)}) %all-to-all-start.1) | async-done | bytes 2097184 | tf_op jit(solution)/shard_map/all_to_all | solution.py:80
  526.5 7.0 all-to-all-start.2
  533.5 0.1 fusion.57
  533.6 3.2 copy.49
  536.8 2.7 copy.50
  539.6 4.1 fusion.20
  543.7 38.8 %all-to-all-done.2 = f32[128,4,1024]{2,1,0:T(4,128)} async-done(((f32[128,4,1024]{2,1,0:T(4,128)}), f32[128,4,1024]{2,1,0:T(4,128)}, u32[]{:S(2)}, u32[]{:S(2)}) %all-to-all-start.2) | async-done | bytes 2097184 | tf_op jit(solution)/shard_map/all_to_all | solution.py:81
  582.4 4.8 copy.53
  587.3 4.3 copy.54
  591.6 4.6 fusion.18
  596.2 2.9 add_bitcast_fusion
  599.1 2.9 subtract_bitcast_fusion
  602.1 0.3 multiply_subtract_fusion.1
  602.3 2.0 fusion.14
  604.3 2.2 fusion.16
  606.5 2.0 convolution_add_fusion
  608.5 2.1 add_bitcast_fusion.1
  610.7 1.3 copy.57
  612.0 6.8 all-to-all-start.3
  618.8 1.3 copy.59
  620.1 25.5 %all-to-all-done.3 = f32[2,256,512]{2,0,1:T(2,128)S(1)} async-done(((f32[2,256,512]{2,0,1:T(2,128)}), f32[2,256,512]{2,0,1:T(2,128)S(1)}, u32[]{:S(2)}, u32[]{:S(2)}) %all-to-all-start.3) | async-done | bytes 1048608 | tf_op jit(solution)/shard_map/all_to_all | solution.py:103
  645.6 7.2 all-to-all-start.4
  652.8 0.3 copy.58
  653.1 0.3 copy.63
  653.5 1.3 fusion.45
  654.7 24.6 %all-to-all-done.4 = f32[2,256,512]{2,0,1:T(2,128)S(1)} async-done(((f32[2,256,512]{2,0,1:T(2,128)}), f32[2,256,512]{2,0,1:T(2,128)S(1)}, u32[]{:S(2)}, u32[]{:S(2)}) %all-to-all-start.4) | async-done | bytes 1048608 | tf_op jit(solution)/shard_map/all_to_all | solution.py:104
  679.4 0.3 copy.60
  679.6 0.3 copy.64
  680.0 1.3 fusion
  681.3 0.7 reshape.131
  682.0 0.1 copy.61
  682.2 33.1 %all_to_all.80 = f32[2,64,4,512]{3,2,0,1:T(4,128)S(1)} all-to-all(f32[2,64,4,512]{3,2,0,1:T(4,128)S(1)} %copy.61), channel_id=1, replica_groups=mesh['seq'=64,'ch'=4] {'seq'}, dimensions={1} | all-to-all | bytes 2097152 | tf_op jit(solution)/shard_map/all_to_all | solution.py:111
  715.3 0.2 squeeze.3
  715.5 0.9 fusion.6
  (21 shorter events, 0.1 us)
Async XLA Ops:
  6.5 329.3 %all-gather.5.cloned.1.call-start = ((), (), s32[]{:S(2)}) async-start(), calls=%async_computation.7 | async-start | bytes 12779520 | tf_op jit(solution)/shard_map/all_gather | solution.py:50
  7.3 358.5 %all-gather.3.cloned.1.call-start = ((), (), s32[]{:S(2)}) async-start(), calls=%async_computation.6 | async-start | bytes 2621440 | tf_op jit(solution)/shard_map/all_gather | solution.py:49
  365.8 11.4 %copy-start.5 = (f32[3,3,512]{2,1,0:T(4,128)S(1)}, f32[3,3,512]{2,1,0:T(4,128)}, u32[]{:S(2)}) copy-start(f32[3,3,512]{2,1,0:T(4,128)} %param.7) | copy-start | bytes 55300
  372.9 5.7 collective-permute-start
  377.3 3.0 copy-start.4
  379.1 1.2 copy-start.1
  385.5 63.3 %all-to-all-start = ((f32[2,64,4,1024]{3,2,0,1:T(4,128)}), f32[2,64,4,1024]{3,2,0,1:T(4,128)S(1)}, u32[]{:S(2)}, u32[]{:S(2)}) async-start(f32[2,64,4,1024]{3,2,0,1:T(4,128)} %copy.43), calls=%async_computation | async-start | bytes 4194304 | tf_op jit(solution)/shard_map/all_to_all | solution.py:68
  470.4 56.1 %all-to-all-start.1 = ((f32[128,4,1024]{2,1,0:T(4,128)}), f32[128,4,1024]{2,1,0:T(4,128)S(1)}, u32[]{:S(2)}, u32[]{:S(2)}) async-start(f32[128,4,1024]{2,1,0:T(4,128)} %copy.48), calls=%async_computation.1 | async-start | bytes 4194304 | tf_op jit(solution)/shard_map/all_to_all | solution.py:80
  526.5 56.0 %all-to-all-start.2 = ((f32[128,4,1024]{2,1,0:T(4,128)}), f32[128,4,1024]{2,1,0:T(4,128)}, u32[]{:S(2)}, u32[]{:S(2)}) async-start(f32[128,4,1024]{2,1,0:T(4,128)} %copy.52), calls=%async_computation.2 | async-start | bytes 4194304 | tf_op jit(solution)/shard_map/all_to_all | solution.py:81
  591.6 4.6 copy-start
  591.6 4.6 copy-start.3
  612.0 33.6 %all-to-all-start.3 = ((f32[2,256,512]{2,0,1:T(2,128)}), f32[2,256,512]{2,0,1:T(2,128)S(1)}, u32[]{:S(2)}, u32[]{:S(2)}) async-start(f32[2,256,512]{2,0,1:T(2,128)} %copy.57), calls=%async_computation.3 | async-start | bytes 2097152 | tf_op jit(solution)/shard_map/all_to_all | solution.py:103
  645.6 33.8 %all-to-all-start.4 = ((f32[2,256,512]{2,0,1:T(2,128)}), f32[2,256,512]{2,0,1:T(2,128)S(1)}, u32[]{:S(2)}, u32[]{:S(2)}) async-start(f32[2,256,512]{2,0,1:T(2,128)} %copy.59), calls=%async_computation.4 | async-start | bytes 2097152 | tf_op jit(solution)/shard_map/all_to_all | solution.py:104
  682.2 33.4 %copy-start.2 = (f32[256,1536]{1,0:T(8,128)S(1)}, f32[256,1536]{1,0:T(8,128)}, u32[]{:S(2)}) copy-start(f32[256,1536]{1,0:T(8,128)} %copy-done.1) | copy-start | bytes 4718596
  682.2 33.4 %copy-start.6 = (f32[512]{0:T(512)S(1)}, f32[512]{0:T(512)}, u32[]{:S(2)}) copy-start(f32[512]{0:T(512)} %param.9) | copy-start | bytes 6148
Sparse Core Ops, SparseCore 0:
  9.1 326.6 all-gather.4
  337.7 28.0 all-gather.2
where the time goes:
time: 729 us; the launch traced here: 724 us
  waiting for transfers between devices  527 us (72%)
  local copies, waits for them, and re-layouts  59.8 us (8%)
  starting transfers between devices  46 us (6%)
  matrix products  41.9 us (6%)
  blocking collectives  33.1 us (5%)
  between operations  14.3 us (2%)
    all_gather x1, waiting for transfers between devices, local(): weight_piece = lax.all_gather(in_weight, 'seq', axis=0, tiled=True)  328 us
    all_to_all x1, waiting for transfers between devices, local(): lax.all_to_all(outgoing, 'seq', split_axis=1, concat_axis=1, tiled=True)  49.4 us
    all_to_all x1, waiting for transfers between devices, local(): lax.all_to_all(turned_real, 'seq', split_axis=0, concat_axis=1, tiled=True)  45 us
    all_to_all x1, waiting for transfers between devices, local(): lax.all_to_all(turned_imag, 'seq', split_axis=0, concat_axis=1, tiled=True)  38.8 us
    all_to_all x1, blocking collectives, local(): lax.all_to_all(leaving, 'seq', split_axis=1, concat_axis=2, tiled=True)  33.1 us
    all_to_all x1, waiting for transfers between devices, local(): lax.all_to_all(back_real, 'seq', split_axis=1, concat_axis=0, tiled=True)  25.5 us
    all_to_all x1, waiting for transfers between devices, local(): lax.all_to_all(back_imag, 'seq', split_axis=1, concat_axis=0, tiled=True)  24.6 us
    dot_general x8, matrix products, along_time(): jnp.einsum('uv,jvc->juc', matrix, values, precision=lax.Precision.HIGHEST...  22.8 us
  transfers between devices with their start and end apart: 8, of which 8 were waited for; matrix products, arithmetic and copies ran while one was open for 5% of the time, Pallas kernels for 0%

commit v1 on v0

v1 whole, which is shorter than its diff:
```python
import math

import jax
import jax.numpy as jnp
import ml_dtypes
import numpy as np
from jax import lax
from jax.experimental import pallas as pl
from jax.experimental.pallas import tpu as pltpu
from jax.sharding import PartitionSpec as P

MESH = pl.DeviceIdType.MESH
BF16, F32 = jnp.bfloat16, jnp.float32

NZ, NY, NX = 8, 4, 4
SEQ, CH = 64, 4
BLOCKS = NZ * NY
TOK = 256
POS = 2 * TOK
FEAT = 1024
HALO = 16
TAPS = 3
WIDTH = 256
COLS = 3 * WIDTH
OWN = 8
WROWS = 64
SPLIT = 48
SIDE = 128
LENGTH = SIDE * SIDE
LO, HI = pl.ds(0, COLS // 2), pl.ds(COLS // 2, COLS // 2)


def split_table(table):
    high = table.astype(ml_dtypes.bfloat16)
    low = (table - high.astype(np.float64)).astype(ml_dtypes.bfloat16)
    return high, low


def tables():
    slot = np.arange(SIDE)
    n1 = 4 * (slot % BLOCKS) + slot // BLOCKS
    k = np.arange(SIDE)
    outer = 2.0 * math.pi * ((np.outer(4 * k + 1, n1)) % 512) / 512.0
    first = np.concatenate([np.cos(outer), -np.sin(outer)], axis=0)
    last = np.concatenate([np.cos(outer).T, -np.sin(outer).T], axis=1) / LENGTH
    inner = 2.0 * math.pi * (np.outer(k, k) % SIDE) / SIDE
    cos, sin = np.cos(inner), np.sin(inner)
    ahead = np.block([[cos, -sin], [sin, cos]])
    back = np.block([[cos, sin], [-sin, cos]])
    twist = 2.0 * math.pi * np.outer(4 * k + 1, k) / (4.0 * LENGTH)
    fh, fl = split_table(first)
    lh, ll = split_table(last)
    return (
        np.concatenate([fh, fh, fl], axis=1),
        np.concatenate([lh, lh, ll], axis=1),
        np.stack(split_table(ahead)),
        np.stack(split_table(back)),
        np.stack([np.cos(twist), np.sin(twist)]).astype(np.float32),
    )


def halves(values):
    high = values.astype(BF16)
    return high, (values - high.astype(F32)).astype(BF16)


def mm(a, b):
    return jnp.dot(a, b, preferred_element_type=F32)


def right_apply(values, table):
    high, low = halves(values)
    return mm(high, table[0]) + mm(low, table[0]) + mm(high, table[1])


def kernel(
    tokens, weights, filt, taps, skip, first, last, ahead, back, twist,
    out,
    w, tok, acc, filt_t, filt_in, gate_t, gate_in, outer_t, outer, y_out, y_in, spec,
    send, recv, many,
):
    seq = lax.axis_index("seq")
    ch = lax.axis_index("ch")
    x_lo, blk = seq % 2, seq // 2
    y, z = blk % NY, blk // NY
    x_hi, core = ch // 2, ch % 2
    x = x_hi * 2 + x_lo

    def seq_of(zz, yy, xx):
        return (zz * NY + yy) * 2 + xx

    def at_yz(dy, dz):
        return {"seq": seq_of((z + dz + NZ) % NZ, (y + dy + NY) % NY, x_lo)}

    def at_x(dx):
        xx = (x + dx + NX) % NX
        return {"seq": seq_of(z, y, xx % 2), "ch": (xx // 2) * 2 + core}

    twin = {"ch": x_hi * 2 + 1 - core}
    mate = {"seq": seq_of(z, y, 1 - x_lo)}

    barrier = pltpu.get_barrier_semaphore()

    def greet(i, _):
        pl.semaphore_signal(barrier, inc=1, device_id={"seq": (seq + i) % SEQ}, device_id_type=MESH)
        return 0

    lax.fori_loop(1, SEQ, greet, 0)
    pl.semaphore_signal(barrier, inc=1, device_id=twin, device_id_type=MESH)
    pl.semaphore_signal(barrier, inc=1, device_id=at_x(3 + 2 * x_lo), device_id_type=MESH)

    started = []
    slots = {}

    def slot(name):
        return slots.setdefault(name, len(slots))

    def go(name, src, dst, device):
        copy = pltpu.make_async_remote_copy(
            src_ref=src, dst_ref=dst, send_sem=send.at[slot(name)], recv_sem=recv.at[slot(name)],
            device_id=device, device_id_type=MESH,
        )
        copy.start()
        started.append(copy)

    def arrived(name, dst):
        pltpu.make_async_copy(dst, dst, recv.at[slot(name)]).wait()

    def local(name, src, dst):
        copy = pltpu.make_async_copy(src, dst, recv.at[slot(name)])
        copy.start()
        return copy

    def block(dy, dz):
        return ((z - dz + NZ) % NZ) * NY + (y - dy + NY) % NY

    def yf(dy, lanes=slice(None)):
        return w.at[block(dy, 0), pl.ds(0, SPLIT), lanes]

    def yf_plane(dz, lanes=slice(None)):
        return w.at[pl.ds(((z - dz + NZ) % NZ) * NY, NY), pl.ds(0, SPLIT), lanes]

    def zf(dy, dz, lanes=slice(None)):
        return w.at[block(dy, dz), pl.ds(SPLIT, 2 * WROWS - SPLIT), lanes]

    def tk(dx, cc, start=0, rows=TOK):
        xx = (x - dx + NX) % NX
        row = pl.multiple_of(HALO + (xx % 2) * TOK + start, 16)
        col = pl.multiple_of(((xx // 2) * 2 + cc) * FEAT, FEAT)
        return tok.at[pl.ds(row, rows), pl.ds(col, FEAT)]

    HALF = TOK // 2

    own_w = local("own_w", weights.at[x_lo], w.at[blk, pl.ds(pl.multiple_of(x_lo * WROWS, WROWS), WROWS)])
    own_tok = local("own_tok", tokens, tk(0, core))
    for i in range(4):
        for j in range(2):
            filt_t[j, i * 128 : (i + 1) * 128, :] = filt[
                j * 128 : (j + 1) * 128, i * 128 : (i + 1) * 128
            ].T
    pl.semaphore_wait(barrier, SEQ + 1)

    other_rows = w.at[blk, pl.ds(pl.multiple_of((1 - x_lo) * WROWS, WROWS), WROWS)]
    go("swap", weights.at[1 - x_lo], w.at[blk, pl.ds(pl.multiple_of(x_lo * WROWS, WROWS), WROWS)], mate)
    go("tok+1", tokens, tk(0, core), at_x(1))
    go("tok-1", tokens, tk(0, core), at_x(-1))
    go("core0", tokens, tk(0, core), twin)

    own_w.wait()
    arrived("swap", other_rows)

    def send_zfy(dz):
        go(f"zfy{dz},+1", zf(0, dz), zf(0, dz), at_yz(1, 0))
        go(f"zfy{dz},-1", zf(0, dz), zf(0, dz), at_yz(-1, 0))

    def pass_zfy(dz):
        arrived(f"zfy{dz},+1", zf(1, dz))
        go(f"zfy{dz},+2", zf(1, dz, LO), zf(1, dz, LO), at_yz(1, 0))
        arrived(f"zfy{dz},-1", zf(-1, dz))
        go(f"zfy{dz},-2", zf(-1, dz, HI), zf(-1, dz, HI), at_yz(-1, 0))

    def end_zfy(dz):
        arrived(f"zfy{dz},+2", zf(2, dz, LO))
        arrived(f"zfy{dz},-2", zf(-2, dz, HI))

    def send_zf(dz):
        far = dz == 3
        for sign, lanes in ((1, LO), (-1, HI)):
            lanes = lanes if far else slice(None)
            ref = zf(0, sign * dz, lanes)
            go(f"zf{sign * (dz + 1)}", ref, ref, at_yz(0, sign))

    def end_zf(dz):
        for sign, lanes in ((1, LO), (-1, HI)):
            arrived(f"zf{sign * dz}", zf(0, sign * dz, lanes if dz == 4 else slice(None)))

    def send_plane(dz):
        far = dz == 3
        for sign, lanes in ((1, LO), (-1, HI)):
            lanes = lanes if far else slice(None)
            ref = yf_plane(sign * dz, lanes)
            go(f"plane{sign * (dz + 1)}", ref, ref, at_yz(0, sign))

    def end_plane(dz):
        for sign, lanes in ((1, LO), (-1, HI)):
            arrived(f"plane{sign * dz}", yf_plane(sign * dz, lanes if dz == 4 else slice(None)))

    def project(dz, fresh=False):
        plane = (z - dz + NZ) % NZ

        def part(i, _):
            cols = pl.ds(pl.multiple_of(i * 256, 256), 256)
            term = mm(
                tok[:, pl.ds(pl.multiple_of(plane * 512, 512), 512)],
                w[pl.ds(plane * NY, NY), :, cols].reshape(512, 256),
            )
            acc[:, cols] = term if fresh else acc[:, cols] + term
            return 0

        lax.fori_loop(0, 3, part, 0)

    go("yf+1", yf(0), yf(0), at_yz(1, 0))
    go("yf-1", yf(0), yf(0), at_yz(-1, 0))
    send_zf(0)
    send_zfy(0)

    arrived("yf+1", yf(1))
    go("yf+2", yf(1, LO), yf(1, LO), at_yz(1, 0))
    arrived("yf-1", yf(-1))
    go("yf-2", yf(-1, HI), yf(-1, HI), at_yz(-1, 0))

    end_zf(1)
    send_zf(1)
    send_zfy(1)
    send_zfy(-1)

    arrived("yf+2", yf(2, LO))
    arrived("yf-2", yf(-2, HI))
    send_plane(0)

    def give_filter(i, _):
        peer = (seq + i) % SEQ
        pltpu.make_async_remote_copy(
            src_ref=filt_t.at[:, pl.ds(pl.multiple_of((peer % 2) * WIDTH + (peer // 2) * OWN, OWN), OWN)],
            dst_ref=filt_in.at[:, pl.ds(pl.multiple_of(seq * OWN, OWN), OWN)],
            send_sem=many.at[0], recv_sem=many.at[1], device_id={"seq": peer}, device_id_type=MESH,
        ).start()
        return 0

    lax.fori_loop(1, SEQ, give_filter, 0)
    pltpu.make_async_copy(
        filt_t.at[:, pl.ds(pl.multiple_of(x_lo * WIDTH + blk * OWN, OWN), OWN)],
        filt_in.at[:, pl.ds(pl.multiple_of(seq * OWN, OWN), OWN)],
        many.at[1],
    ).start()

    pass_zfy(0)
    end_zf(2)
    send_zf(2)
    send_zfy(2)
    send_zfy(-2)
    end_zf(3)
    send_zf(3)
    send_zfy(3)
    send_zfy(-3)
    pass_zfy(1)
    pass_zfy(-1)
    end_zf(4)
    send_zfy(4)

    arrived("tok+1", tk(1, core))
    go("tok+2", tk(1, core, 0, HALF), tk(1, core, 0, HALF), at_x(1))
    go("core+1", tk(1, core), tk(1, core), twin)
    arrived("tok-1", tk(-1, core))
    go("tok-2", tk(-1, core, HALF, HALF), tk(-1, core, HALF, HALF), at_x(-1))
    go("core-1", tk(-1, core), tk(-1, core), twin)

    end_plane(1)
    send_plane(1)
    pass_zfy(2)
    pass_zfy(-2)

    arrived("tok+2", tk(2, core, 0, HALF))
    go("core+2", tk(2, core, 0, HALF), tk(2, core, 0, HALF), twin)
    arrived("tok-2", tk(2, core, HALF, HALF))
    go("core-2", tk(2, core, HALF, HALF), tk(2, core, HALF, HALF), twin)
    own_tok.wait()
    arrived("core0", tk(0, 1 - core))
    arrived("core+1", tk(1, 1 - core))
    arrived("core-1", tk(-1, 1 - core))
    arrived("core+2", tk(2, 1 - core, 0, HALF))
    arrived("core-2", tk(2, 1 - core, HALF, HALF))
    after = (blk + 1) % BLOCKS
    go("halo", tok.at[pl.ds(POS, HALO)], tok.at[pl.ds(0, HALO)], {"seq": after * 2 + x_lo})

    end_zfy(0)
    pass_zfy(3)
    pass_zfy(-3)
    end_plane(2)
    send_plane(2)
    arrived("halo", tok.at[pl.ds(0, HALO)])
    project(0, fresh=True)
    end_zfy(1)
    end_zfy(-1)
    project(1)
    project(-1)
    pass_zfy(4)
    end_plane(3)
    send_plane(3)

    def transform(load, pair):
        columns = jnp.concatenate([load(2 * pair), load(2 * pair + 1)], axis=1)
        high, low = halves(columns)
        turned = mm(first[...], jnp.concatenate([high, low, high], axis=0))
        cos, sin = twist[0], twist[1]
        rows = []
        for i in range(2):
            real = turned[:SIDE, i * SIDE : (i + 1) * SIDE]
            imag = turned[SIDE:, i * SIDE : (i + 1) * SIDE]
            rows.append(jnp.concatenate([real * cos + imag * sin, imag * cos - real * sin], axis=1))
        return right_apply(jnp.concatenate(rows, axis=0), ahead)

    def load_filter(c):
        return jnp.concatenate(
            [
                filt_in[j % 2, pl.ds(c + OWN * (j // 2), BLOCKS, stride=2 * OWN), :]
                for j in range(4)
            ],
            axis=0,
        )

    def load_gate(c):
        return jnp.concatenate(
            [gate_in[j, pl.ds(c, BLOCKS, stride=OWN), :] for j in range(4)], axis=0
        )

    pltpu.make_async_copy(filt_in, filt_in, many.at[1]).wait()
    for pair in range(OWN // 2):
        spec[pair * 256 : (pair + 1) * 256, :] = transform(load_filter, pair)

    end_zfy(2)
    end_zfy(-2)
    project(2)
    project(-2)
    end_zfy(3)
    end_zfy(-3)
    project(3)
    project(-3)
    end_plane(4)
    end_zfy(4)
    project(4)

    acc[8:16, :] = jnp.where(blk == 0, 0.0, acc[8:16, :])
    taps_col = pl.ds(pl.multiple_of(x_lo * WIDTH, WIDTH), WIDTH)
    tap = [[taps[pl.ds(3 * j + s, 1), taps_col] for s in range(3)] for j in range(TAPS)]
    for lane in range(2):
        for row in range(4):

            def short(s):
                total = None
                for j in range(TAPS):
                    cols = slice(s * WIDTH + lane * 128, s * WIDTH + (lane + 1) * 128)
                    start = HALO - j + row * 128
                    term = tap[j][s][:, lane * 128 : (lane + 1) * 128] * acc[start : start + 128, cols]
                    total = term if total is None else total + term
                return total

            place = (row, slice(lane * 128, (lane + 1) * 128))
            gate_t[place] = (short(1) * short(2)).T
            outer_t[place] = short(0).T

    def give_gate(i, _):
        peer = (blk + i) % BLOCKS
        pltpu.make_async_remote_copy(
            src_ref=gate_t.at[:, pl.ds(pl.multiple_of(peer * OWN, OWN), OWN)],
            dst_ref=gate_in.at[:, pl.ds(pl.multiple_of(blk * OWN, OWN), OWN)],
            send_sem=many.at[2], recv_sem=many.at[3], device_id={"seq": peer * 2 + x_lo}, device_id_type=MESH,
        ).start()
        return 0

    lax.fori_loop(1, BLOCKS, give_gate, 0)
    pltpu.make_async_copy(
        gate_t.at[:, pl.ds(pl.multiple_of(blk * OWN, OWN), OWN)],
        gate_in.at[:, pl.ds(pl.multiple_of(blk * OWN, OWN), OWN)],
        many.at[3],
    ).start()
    mine = pl.ds(pl.multiple_of(x_lo * WIDTH, WIDTH), WIDTH)
    theirs = pl.ds(pl.multiple_of((1 - x_lo) * WIDTH, WIDTH), WIDTH)
    go("outer", outer_t.at[pl.ds(2 * (1 - x_lo), 2)], outer.at[:, mine], mate)
    own_outer = local("own_outer", outer_t.at[pl.ds(2 * x_lo, 2)], outer.at[:, mine])
    pltpu.make_async_copy(gate_in, gate_in, many.at[3]).wait()

    for pair in range(OWN // 2):
        spectrum = transform(load_gate, pair)
        response = spec[pair * 256 : (pair + 1) * 256, :]
        sr, si = spectrum[:, :SIDE], spectrum[:, SIDE:]
        rr, ri = response[:, :SIDE], response[:, SIDE:]
        product = jnp.concatenate([sr * rr - si * ri, sr * ri + si * rr], axis=1)
        inverse = right_apply(product, back)
        cos, sin = twist[0], twist[1]
        cols = []
        for i in range(2):
            real = inverse[i * SIDE : (i + 1) * SIDE, :SIDE]
            imag = inverse[i * SIDE : (i + 1) * SIDE, SIDE:]
            cols.append(jnp.concatenate([real * cos - imag * sin, imag * cos + real * sin], axis=0))
        high, low = halves(jnp.concatenate(cols, axis=1))
        result = mm(last[...], jnp.concatenate([high, low, high], axis=0))
        for i in range(2):
            c = 2 * pair + i
            gain = skip[x_lo * WIDTH + blk * OWN + c]
            total = result[:, i * SIDE : (i + 1) * SIDE] + gain * load_gate(c)
            for j in range(4):
                y_out[j, pl.ds(c, BLOCKS, stride=OWN), :] = total[j * BLOCKS : (j + 1) * BLOCKS, :]

    rows_here = pl.ds(pl.multiple_of(x_lo * WIDTH + blk * OWN, OWN), OWN)

    def chunk(peer):
        return y_out.at[pl.ds((peer % 2) * 2, 2), pl.ds(pl.multiple_of((peer // 2) * OWN, OWN), OWN)]

    def give_y(i, _):
        peer = (seq + i) % SEQ
        pltpu.make_async_remote_copy(
            src_ref=chunk(peer), dst_ref=y_in.at[:, rows_here],
            send_sem=many.at[4], recv_sem=many.at[5], device_id={"seq": peer}, device_id_type=MESH,
        ).start()
        return 0

    lax.fori_loop(1, SEQ, give_y, 0)
    pltpu.make_async_copy(chunk(seq), y_in.at[:, rows_here], many.at[5]).start()
    own_outer.wait()
    arrived("outer", outer.at[:, theirs])
    pltpu.make_async_copy(y_in, y_in, many.at[5]).wait()
    for i in range(4):
        for j in range(2):
            place = (j, slice(i * 128, (i + 1) * 128))
            out[j * 128 : (j + 1) * 128, i * 128 : (i + 1) * 128] = (outer[place] * y_in[place]).T

    for copy in started:
        copy.wait_send()
    sent = filt_t.at[:, pl.ds(OWN, (SEQ - 1) * OWN)]
    pltpu.make_async_copy(sent, sent, many.at[0]).wait()
    sent = gate_t.at[:, pl.ds(OWN, (BLOCKS - 1) * OWN)]
    pltpu.make_async_copy(sent, sent, many.at[2]).wait()
    sent = y_in.at[:, pl.ds(OWN, (SEQ - 1) * OWN)]
    pltpu.make_async_copy(sent, sent, many.at[4]).wait()


SLOTS = 80


def local(tokens, in_weight, short_filter, long_filter, skip_gain):
    width = skip_gain.shape[0]
    weights = in_weight.reshape(WROWS, 3, 2, WIDTH).transpose(2, 0, 1, 3).reshape(2, WROWS, COLS)
    taps = short_filter.reshape(3 * TAPS, width)
    vmem = pl.BlockSpec(memory_space=pltpu.VMEM)
    anywhere = pl.BlockSpec(memory_space=pl.ANY)
    out = pl.pallas_call(
        kernel,
        out_shape=jax.ShapeDtypeStruct((TOK, width), F32),
        in_specs=[anywhere, anywhere, vmem, vmem, pl.BlockSpec(memory_space=pltpu.SMEM)] + [vmem] * 5,
        out_specs=vmem,
        scratch_shapes=[
            pltpu.VMEM((BLOCKS, 2 * WROWS, COLS), BF16),
            pltpu.VMEM((HALO + POS, CH * FEAT), BF16),
            pltpu.VMEM((HALO + POS, COLS), F32),
            pltpu.VMEM((2, 2 * WIDTH, SIDE), F32),
            pltpu.VMEM((2, 2 * WIDTH, SIDE), F32),
            pltpu.VMEM((4, WIDTH, SIDE), F32),
            pltpu.VMEM((4, WIDTH, SIDE), F32),
            pltpu.VMEM((4, WIDTH, SIDE), F32),
            pltpu.VMEM((2, 2 * WIDTH, SIDE), F32),
            pltpu.VMEM((4, WIDTH, SIDE), F32),
            pltpu.VMEM((2, 2 * WIDTH, SIDE), F32),
            pltpu.VMEM((OWN * SIDE, 2 * SIDE), F32),
            pltpu.SemaphoreType.DMA((SLOTS,)),
            pltpu.SemaphoreType.DMA((SLOTS,)),
            pltpu.SemaphoreType.DMA((6,)),
        ],
        compiler_params=pltpu.CompilerParams(
            collective_id=0, has_side_effects=True, vmem_limit_bytes=40 * 1024 * 1024
        ),
    )(tokens, weights, long_filter, taps, skip_gain, *tables())
    return out.astype(BF16)


def solution(mesh):
    placed = (P("seq", "ch"), P("seq", None, "ch"), P(None, None, "ch"), P("seq", "ch"), P("ch"))
    return jax.shard_map(
        local, mesh=mesh, in_specs=placed, out_specs=P("seq", "ch"), check_vma=False
    )
```

time: 729 us -> 117 us (0.16)
  waiting for transfers between devices: 527 us -> 0 us
  Pallas kernels: 0 us -> 107 us
  local copies, waits for them, and re-layouts: 59.8 us -> 6.65 us
  starting transfers between devices: 46 us -> 0 us
  matrix products: 41.9 us -> 0 us
  blocking collectives: 33.1 us -> 0 us
  between operations: 14.3 us -> 0.07 us
    all_gather x2 -> x0, waiting for transfers between devices: 341 us -> none  [the longest x1 328 us: local(): weight_piece = lax.all_gather(in_weight, 'seq', axis=0, tiled=True)]
    all_to_all x5 -> x0, waiting for transfers between devices: 183 us -> none  [the longest x1 49.4 us: local(): lax.all_to_all(outgoing, 'seq', split_axis=1, concat_axis=1, tiled=True)]
    pallas_call x0 -> x1, Pallas kernels: none -> 107 us  [local(): pl.pallas_call(kernel, out_shape=jax.ShapeDtypeStruct((TOK, width), F32),...]
    dot_general x13 -> x0, matrix products: 41.9 us -> none  [the longest x8 22.8 us: along_time(): jnp.einsum('uv,jvc->juc', matrix, values, precision=lax.Precision.HIGHEST...]
    all_to_all x5 -> x0, starting transfers between devices: 41.7 us -> none  [the longest x1 13.8 us: local(): lax.all_to_all(outgoing, 'seq', split_axis=1, concat_axis=1, tiled=True)]
    all_to_all x1 -> x0, blocking collectives: 33.1 us -> none  [local(): lax.all_to_all(leaving, 'seq', split_axis=1, concat_axis=2, tiled=True)]
    all_gather x1 -> x0, local copies, waits for them, and re-layouts: 17.1 us -> none  [local(): weight_piece = lax.all_gather(in_weight, 'seq', axis=0, tiled=True)]
    all_to_all x7 -> x0, local copies, waits for them, and re-layouts: 15.8 us -> none  [the longest x2 9.16 us: local(): lax.all_to_all(turned_imag, 'seq', split_axis=0, concat_axis=1, tiled=True)]
  transfers between devices with their start and end apart: 8 -> 0, of which waited for: 8 -> 0; matrix products, arithmetic and copies ran while one was open for 5% -> 0% of each run, Pallas kernels for 0% -> 0%
where the time goes in v1:
time: 117 us; the launch traced here: 115 us
  Pallas kernels  107 us (91%)
  local copies, waits for them, and re-layouts  6.65 us (6%)
    pallas_call x1, Pallas kernels, local(): pl.pallas_call(kernel, out_shape=jax.ShapeDtypeStruct((TOK, width), F32),...  107 us
    unnamed x16, local copies, waits for them, and re-layouts  4.46 us

profile of v1, /device:TPU:2, one launch (start us, length us, event | category | flops | bytes accessed | tf_op | source)
XLA Modules:
  0.0 114.9 jit_solution(3683987046974992959)
XLA Ops:
  0.0 0.0 copy-start.7
  0.0 0.8 reshape.11.taps
  0.8 0.0 copy-start.1
  0.8 1.0 reshape.9
  1.8 0.0 copy-start
  1.8 0.2 copy.14
  2.0 0.0 copy-start.2
  2.0 0.2 reshape.10.weights
  2.2 0.0 copy-done.7
  2.3 0.0 copy-done.1
  2.3 0.6 copy-done
  2.9 0.1 copy-done.2
  3.0 0.0 copy-start.3
  3.0 0.9 copy-done.3
  4.0 0.0 copy-start.4
  4.0 0.9 copy-done.4
  4.9 0.0 copy-start.5
  4.9 0.9 copy-done.5
  5.8 0.0 copy-start.6
  5.8 0.9 copy-done.6
  6.7 107.4 %shard_map.100 = f32[256,512]{1,0:T(8,128)S(1)} custom-call(bf16[256,1024]{1,0:T(8,128)(2,1)S(1)} %copy-done, bf16[2,64,768]{2,1,0:T(8,128)(2,1)S(1)} %reshape.10.weights, f32[256,512]{1,0:T(8,128)S(1)} %copy-done.1, f32[9,512]{1,0:T(8,128)S(1)} %reshape.11.taps, f32[512]{0:T(512)S(1)} %copy-done.7, bf16[256,384]{1,0:T(8,128)(2,1)S(1)} %copy-done.5, ...), custom_call_target="tpu_custom_call" | custom-call | tf_op jit(solution)/shard_map/pallas_call | solution.py:457
  114.1 0.7 convert_element_type.3
Async XLA Ops:
  0.0 2.2 %copy-start.7 = (f32[512]{0:T(512)S(1)}, f32[512]{0:T(512)}, u32[]{:S(2)}) copy-start(f32[512]{0:T(512)} %skip.1) | copy-start | bytes 6148
  0.8 1.5 %copy-start.1 = (f32[256,512]{1,0:T(8,128)S(1)}, f32[256,512]{1,0:T(8,128)}, u32[]{:S(2)}) copy-start(f32[256,512]{1,0:T(8,128)} %filt.1) | copy-start | bytes 1572868
  1.8 1.1 copy-start
  2.0 1.0 copy-start.2
  3.0 0.9 copy-start.3
  4.0 0.9 copy-start.4
  4.9 0.9 copy-start.5
  5.8 0.9 copy-start.6

commit v2 on v1

v2 whole, which is shorter than its diff:
```python
import math

import jax
import jax.numpy as jnp
import ml_dtypes
import numpy as np
from jax import lax
from jax.experimental import pallas as pl
from jax.experimental.pallas import tpu as pltpu
from jax.sharding import PartitionSpec as P

MESH = pl.DeviceIdType.MESH
BF16, F32 = jnp.bfloat16, jnp.float32

NZ, NY, NX = 8, 4, 4
AROUND = (1, -1, 2, -2)
SEQ, CH = 64, 4
BLOCKS = NZ * NY
TOK = 256
POS = 2 * TOK
FEAT = 1024
HALO = 16
TAPS = 3
WIDTH = 256
COLS = 3 * WIDTH
OWN = 8
WROWS = 64
SPLIT = 48
SIDE = 128
LENGTH = SIDE * SIDE
SPREAD = 27
LO, HI = pl.ds(0, WIDTH // 2), pl.ds(WIDTH // 2, WIDTH // 2)
REST = 2 * WROWS - SPLIT


SWAP, ZF_OWN, ZF_ADDED, ZF, ZFY_OWN, ZFY_ADDED, ZFY, YF, PLANE, TOKEN, CORE, LAST_ROWS, TURN, GIVE, RESPOND, PROJECT = range(16)


def key(kind, first=0, second=0):
    return 100 * kind + 10 * (first + 4) + second + 4


STEPS = (
    44, 454, 434, 134, 154, 1244, 1044, 954, 934, 1304, 1314, 534, 554, 254, 734, 754, 234, 1324, 642, 646, 655,
    653, 364, 633, 635, 324, 1334, 724, 764, 1344, 1354, 1054, 964, 856, 834, 835, 836, 857, 855, 837, 854, 1034,
    924, 1364, 665, 663, 625, 623, 314, 374, 652, 656, 632, 636, 1064, 1024, 1144, 866, 824, 825, 826, 867, 865,
    827, 864, 1444, 662, 626, 622, 666, 615, 613, 304, 675, 673, 384, 1544, 1554, 1534, 876, 814, 815, 877, 875,
    817, 874, 816, 1564, 685, 683, 1524, 612, 672, 616, 676, 886, 804, 805, 887, 885, 884, 806, 807, 682, 686, 1514,
    1574, 1584,
)


def split_table(table):
    high = table.astype(ml_dtypes.bfloat16)
    low = (table - high.astype(np.float64)).astype(ml_dtypes.bfloat16)
    return high, low


def tables():
    slot = np.arange(SIDE)
    n1 = 4 * (slot % BLOCKS) + slot // BLOCKS
    k = np.arange(SIDE)
    outer = 2.0 * math.pi * ((np.outer(4 * k + 1, n1)) % 512) / 512.0
    first = np.concatenate([np.cos(outer), -np.sin(outer)], axis=0)
    last = np.concatenate([np.cos(outer).T, -np.sin(outer).T], axis=1) / LENGTH
    inner = 2.0 * math.pi * (np.outer(k, k) % SIDE) / SIDE
    cos, sin = np.cos(inner), np.sin(inner)
    ahead = np.block([[cos, -sin], [sin, cos]])
    back = np.block([[cos, sin], [-sin, cos]])
    twist = 2.0 * math.pi * np.outer(4 * k + 1, k) / (4.0 * LENGTH)
    fh, fl = split_table(first)
    lh, ll = split_table(last)
    return (
        np.concatenate([fh, fh, fl], axis=1),
        np.concatenate([lh, lh, ll], axis=1),
        np.stack(split_table(ahead)),
        np.stack(split_table(back)),
        np.stack([np.cos(twist), np.sin(twist)]).astype(np.float32),
    )


def halves(values):
    high = values.astype(BF16)
    return high, (values - high.astype(F32)).astype(BF16)


def mm(a, b):
    return jnp.dot(a, b, preferred_element_type=F32)


def right_apply(values, table):
    high, low = halves(values)
    return mm(high, table[0]) + mm(low, table[0]) + mm(high, table[1])


def kernel(
    tokens, weights, filt_hbm, taps_hbm, skip_hbm, first_hbm, last_hbm, ahead_hbm, back_hbm, twist_hbm,
    out,
    filt, taps, skip, first, last, ahead, back, twist,
    w, tok, acc, filt_t, filt_in, gate_t, gate_in, outer_t, outer, y_out, y_in, spec,
    send, recv, many,
):
    seq = lax.axis_index("seq")
    ch = lax.axis_index("ch")
    x_lo, blk = seq % 2, seq // 2
    y, z = blk % NY, blk // NY
    x_hi, core = ch // 2, ch % 2
    x = x_hi * 2 + x_lo

    def seq_of(zz, yy, xx):
        return (zz * NY + yy) * 2 + xx

    def at_yz(dy, dz):
        return {"seq": seq_of((z + dz + NZ) % NZ, (y + dy + NY) % NY, x_lo)}

    def at_x(dx):
        xx = (x + dx + NX) % NX
        return {"seq": seq_of(z, y, xx % 2), "ch": (xx // 2) * 2 + core}

    twin = {"ch": x_hi * 2 + 1 - core}
    mate = {"seq": seq_of(z, y, 1 - x_lo)}

    started = []
    slots = {}

    def slot(name):
        return slots.setdefault(name, len(slots))

    def go(name, src, dst, device):
        copy = pltpu.make_async_remote_copy(
            src_ref=src, dst_ref=dst, send_sem=send.at[slot(name)], recv_sem=recv.at[slot(name)],
            device_id=device, device_id_type=MESH,
        )
        copy.start()
        started.append(copy)

    def arrived(name, dst):
        pltpu.make_async_copy(dst, dst, recv.at[slot(name)]).wait()

    def local(name, src, dst):
        copy = pltpu.make_async_copy(src, dst, recv.at[slot(name)])
        copy.start()
        return copy

    def block(dy, dz):
        return ((z - dz + NZ) % NZ) * NY + (y - dy + NY) % NY

    early = pl.multiple_of(x_lo * SPLIT, 16)
    late = pl.multiple_of((1 - x_lo) * REST, 16)
    own_rows = pl.ds(pl.multiple_of(x_lo * WROWS, WROWS), WROWS)
    mate_rows = pl.ds(pl.multiple_of((1 - x_lo) * WROWS, WROWS), WROWS)
    added_rows = pl.ds(pl.multiple_of(x_lo * SPLIT + (1 - x_lo) * WROWS, 16), REST - WROWS)

    def yf(dy, lanes=slice(None)):
        return w.at[block(dy, 0), :, pl.ds(late, SPLIT), lanes]

    def yf_plane(dz, piece, lanes=slice(None)):
        return w.at[((z - dz + NZ) % NZ) * NY + piece, :, pl.ds(late, SPLIT), lanes]

    def zf(dy, dz, lanes=slice(None), rows=pl.ds(early, REST)):
        return w.at[block(dy, dz), :, rows, lanes]

    def tk(dx, cc, start=0, rows=TOK):
        xx = (x - dx + NX) % NX
        row = pl.multiple_of(HALO + (xx % 2) * TOK + start, 16)
        col = pl.multiple_of(((xx // 2) * 2 + cc) * FEAT, FEAT)
        return tok.at[pl.ds(row, rows), pl.ds(col, FEAT)]

    HALF = TOK // 2

    mine = pl.ds(pl.multiple_of(x_lo * WIDTH, WIDTH), WIDTH)
    theirs = pl.ds(pl.multiple_of((1 - x_lo) * WIDTH, WIDTH), WIDTH)
    own_w = local(-1, weights.at[:, :, mine], w.at[blk, :, own_rows])
    own_filt = local(-2, filt_hbm, filt)
    own_tok = local(-3, tokens, tk(0, core))
    tables_in = [
        local(name, src, dst)
        for name, src, dst in (
            (-5, first_hbm, first), (-6, last_hbm, last), (-7, ahead_hbm, ahead), (-8, back_hbm, back),
            (-9, twist_hbm, twist), (-10, taps_hbm, taps), (-11, skip_hbm, skip),
        )
    ]

    barrier = pltpu.get_barrier_semaphore()

    def greet(i, _):
        pl.semaphore_signal(barrier, inc=1, device_id={"seq": (seq + i) % SEQ}, device_id_type=MESH)
        return 0

    lax.fori_loop(1, SEQ, greet, 0)
    pl.semaphore_signal(barrier, inc=1, device_id=twin, device_id_type=MESH)
    pl.semaphore_signal(barrier, inc=1, device_id=at_x(3 + 2 * x_lo), device_id_type=MESH)
    pl.semaphore_wait(barrier, SEQ + 1)

    own_w.wait()

    copies = {}

    def plan(name, src, device, after, comes, dst=None):
        copies[name] = (src, src if dst is None else dst, device, after, comes)

    def zf_parts(dz):
        if dz == 0:
            return [key(SWAP)]
        if abs(dz) == 1:
            return [key(ZF_OWN, dz), key(ZF_ADDED, dz)]
        return [key(ZF, 4), key(ZF, -4)] if dz == 4 else [key(ZF, dz)]

    everything = slice(None)
    plan(key(SWAP), weights.at[:, :, theirs], mate, [], w.at[blk, :, mate_rows], w.at[blk, :, own_rows])
    for sign, lanes in ((1, LO), (-1, HI)):
        for own, own_y, rows, after in (
            (ZF_OWN, ZFY_OWN, own_rows, []), (ZF_ADDED, ZFY_ADDED, added_rows, [key(SWAP)]),
        ):
            ref = zf(0, 0, rows=rows)
            plan(key(own, sign), ref, at_yz(0, sign), after, zf(0, sign, rows=rows))
            plan(key(own_y, sign), ref, at_yz(sign, 0), after, zf(sign, 0, rows=rows))
        for dz in (2, 3, 4):
            part = lanes if dz == 4 else everything
            far = sign * dz
            plan(key(ZF, far), zf(0, far - sign, part), at_yz(0, sign), zf_parts(far - sign), zf(0, far, part))
        for dz in range(-3, 5):
            after = [key(ZFY_OWN, sign), key(ZFY_ADDED, sign)]
            if dz != 0:
                after = [key(ZFY, dz, sign)]
                plan(after[0], zf(0, dz), at_yz(sign, 0), zf_parts(dz), zf(sign, dz))
            plan(key(ZFY, dz, 2 * sign), zf(sign, dz, lanes), at_yz(sign, 0), after, zf(2 * sign, dz, lanes))
        plan(key(YF, sign), yf(0), at_yz(sign, 0), [key(SWAP)], yf(sign))
        plan(key(YF, 2 * sign), yf(sign, lanes), at_yz(sign, 0), [key(YF, sign)], yf(2 * sign, lanes))
        for dz in (1, 2, 3, 4):
            part = lanes if dz == 4 else everything
            for piece in range(NY):
                near = sign * (dz - 1)
                after = [key(PLANE, near, piece)] if dz > 1 else [key(YF, by) for by in AROUND]
                plan(
                    key(PLANE, sign * dz, piece), yf_plane(near, piece, part), at_yz(0, sign), after,
                    yf_plane(sign * dz, piece, part),
                )
        start = 0 if sign == 1 else HALF
        plan(key(TOKEN, sign), tokens, at_x(sign), [], tk(sign, core), tk(0, core))
        plan(
            key(TOKEN, 2 * sign), tk(sign, core, start, HALF), at_x(sign), [key(TOKEN, sign)],
            tk(2, core, start, HALF),
        )
        plan(key(CORE, sign), tk(sign, core), twin, [key(TOKEN, sign)], tk(sign, 1 - core))
        plan(
            key(CORE, 2 * sign), tk(2, core, start, HALF), twin, [key(TOKEN, 2 * sign)],
            tk(2, 1 - core, start, HALF),
        )
    plan(key(CORE), tokens, twin, [], tk(0, 1 - core), tk(0, core))
    after = (blk + 1) % BLOCKS
    all_tok = [key(kind, by) for kind in (TOKEN, CORE) for by in AROUND] + [key(CORE)]
    halo = tok.at[pl.ds(0, HALO)]
    plan(key(LAST_ROWS), tok.at[pl.ds(POS, HALO)], {"seq": after * 2 + x_lo}, all_tok, halo, halo)

    here = set()

    def need(names):
        for name in names:
            if name not in here:
                arrived(name, copies[name][4])
                here.add(name)

    def plane_parts(dz):
        parts = zf_parts(dz) + [key(ZFY, dz, by) for by in (2, -2)]
        if dz == 0:
            near = [key(kind, by) for kind in (ZFY_OWN, ZFY_ADDED) for by in (1, -1)]
            return parts + near + [key(YF, by) for by in AROUND]
        ends = (4, -4) if dz == 4 else (dz,)
        parts += [key(ZFY, dz, by) for by in (1, -1)]
        return parts + [key(PLANE, end, piece) for end in ends for piece in range(NY)]

    def project(dz, fresh=False):
        plane = (z - dz + NZ) % NZ

        def part(i, _):
            cols = pl.ds(pl.multiple_of(i * 256, 256), 256)
            term = mm(
                tok[:, pl.ds(pl.multiple_of(plane * 512, 512), 512)],
                w[pl.ds(plane * NY, NY), i].reshape(512, 256),
            )
            acc[:, cols] = term if fresh else acc[:, cols] + term
            return 0

        lax.fori_loop(0, 3, part, 0)

    def rows8(index):
        return pl.ds(pl.multiple_of(index * 8, 8), 8)

    def rows16(index):
        return pl.ds(pl.multiple_of(index * 16, 16), 16)

    def turn_filter():
        own_filt.wait()
        for i in range(4):
            for j in range(2):
                filt_t[i % 2, pl.ds((i // 2) * WIDTH + j, SIDE, stride=2), :] = filt[
                    j * 128 : (j + 1) * 128, i * 128 : (i + 1) * 128
                ].T
        pltpu.make_async_copy(filt_t.at[:, rows8(x_lo * BLOCKS + blk)], filt_in.at[:, rows8(seq)], many.at[1]).start()

    def give_filter(part):
        def give(i, _):
            peer = (seq + SPREAD * i) % SEQ
            pltpu.make_async_remote_copy(
                src_ref=filt_t.at[:, rows8((peer % 2) * BLOCKS + peer // 2)], dst_ref=filt_in.at[:, rows8(seq)],
                send_sem=many.at[0], recv_sem=many.at[1], device_id={"seq": peer}, device_id_type=MESH,
            ).start()
            return 0

        lax.fori_loop(1 + 9 * part, 10 + 9 * part, give, 0)

    def transform(load, pair):
        columns = jnp.concatenate([load(2 * pair), load(2 * pair + 1)], axis=1)
        high, low = halves(columns)
        turned = mm(first[...], jnp.concatenate([high, low, high], axis=0))
        cos, sin = twist[0], twist[1]
        rows = []
        for i in range(2):
            real = turned[:SIDE, i * SIDE : (i + 1) * SIDE]
            imag = turned[SIDE:, i * SIDE : (i + 1) * SIDE]
            rows.append(jnp.concatenate([real * cos + imag * sin, imag * cos - real * sin], axis=1))
        return right_apply(jnp.concatenate(rows, axis=0), ahead)

    def load_filter(c):
        return jnp.concatenate(
            [
                filt_in[c // 4, pl.ds(8 * (j // 2) + 2 * (c % 4) + j % 2, BLOCKS, stride=16), :]
                for j in range(4)
            ],
            axis=0,
        )

    def load_gate(c):
        return jnp.concatenate(
            [gate_in[c // 4, pl.ds(4 * (c % 4) + j, BLOCKS, stride=16), :] for j in range(4)], axis=0
        )

    def respond():
        for copy in tables_in:
            copy.wait()
        pltpu.make_async_copy(filt_in, filt_in, many.at[1]).wait()
        for pair in range(OWN // 2):
            spec[pair * 256 : (pair + 1) * 256, :] = transform(load_filter, pair)

    fresh = True
    for step in STEPS:
        kind, number = step // 100, step // 10 % 10 - 4
        if step in copies:
            src, dst, device, after, _ = copies[step]
            need(after)
            if kind == LAST_ROWS:
                own_tok.wait()
            go(step, src, dst, device)
        elif kind == PROJECT:
            need([key(LAST_ROWS)] if fresh else [])
            need(plane_parts(number))
            project(number, fresh)
            fresh = False
        elif kind == GIVE:
            give_filter(number + 4)
        elif kind == TURN:
            turn_filter()
        else:
            respond()
    assert here == set(copies)

    acc[8:16, :] = jnp.where(blk == 0, 0.0, acc[8:16, :])
    taps_col = pl.ds(pl.multiple_of(x_lo * WIDTH, WIDTH), WIDTH)
    tap = [[taps[j, pl.ds(s, 1), taps_col] for s in range(3)] for j in range(TAPS)]

    def give_gate(half):
        def give(i, _):
            peer = (blk + SPREAD * i) % BLOCKS
            pltpu.make_async_remote_copy(
                src_ref=gate_t.at[half, rows16(peer)], dst_ref=gate_in.at[half, rows16(blk)],
                send_sem=many.at[2], recv_sem=many.at[3 + half], device_id={"seq": peer * 2 + x_lo},
                device_id_type=MESH,
            ).start()
            return 0

        lax.fori_loop(1, BLOCKS, give, 0)
        pltpu.make_async_copy(gate_t.at[half, rows16(blk)], gate_in.at[half, rows16(blk)], many.at[3 + half]).start()

    for half in range(2):
        lanes = slice(half * SIDE, (half + 1) * SIDE)
        for row in range(4):

            def short(s):
                total = None
                for j in range(TAPS):
                    start = HALO - j + row * SIDE
                    cols = slice(s * WIDTH + half * SIDE, s * WIDTH + (half + 1) * SIDE)
                    term = tap[j][s][:, lanes] * acc[start : start + SIDE, cols]
                    total = term if total is None else total + term
                return total

            gate_t[half, pl.ds(row, SIDE, stride=4), :] = (short(1) * short(2)).T
            outer_t[row, lanes, :] = short(0).T
        give_gate(half)
    go(-4, outer_t.at[pl.ds(2 * (1 - x_lo), 2)], outer.at[:, mine], mate)
    own_outer = local(-12, outer_t.at[pl.ds(2 * x_lo, 2)], outer.at[:, mine])

    def convolve(pair):
        spectrum = transform(load_gate, pair)
        response = spec[pair * 256 : (pair + 1) * 256, :]
        sr, si = spectrum[:, :SIDE], spectrum[:, SIDE:]
        rr, ri = response[:, :SIDE], response[:, SIDE:]
        product = jnp.concatenate([sr * rr - si * ri, sr * ri + si * rr], axis=1)
        inverse = right_apply(product, back)
        cos, sin = twist[0], twist[1]
        cols = []
        for i in range(2):
            real = inverse[i * SIDE : (i + 1) * SIDE, :SIDE]
            imag = inverse[i * SIDE : (i + 1) * SIDE, SIDE:]
            cols.append(jnp.concatenate([real * cos - imag * sin, imag * cos + real * sin], axis=0))
        high, low = halves(jnp.concatenate(cols, axis=1))
        result = mm(last[...], jnp.concatenate([high, low, high], axis=0))
        for i in range(2):
            c = 2 * pair + i
            gain = skip[x_lo * WIDTH + (c // 4) * SIDE + blk * 4 + c % 4]
            total = result[:, i * SIDE : (i + 1) * SIDE] + gain * load_gate(c)
            for j in range(4):
                place = pl.ds(8 * (j // 2) + 2 * (c % 4) + j % 2, BLOCKS, stride=16)
                y_out[c // 4, place, :] = total[j * BLOCKS : (j + 1) * BLOCKS, :]

    def give_y(half):
        here8 = rows8(x_lo * BLOCKS + blk)

        def give(i, _):
            peer = (seq + SPREAD * i) % SEQ
            pltpu.make_async_remote_copy(
                src_ref=y_out.at[half, rows8(peer)], dst_ref=y_in.at[half, here8],
                send_sem=many.at[5], recv_sem=many.at[6 + half], device_id={"seq": peer}, device_id_type=MESH,
            ).start()
            return 0

        lax.fori_loop(1, SEQ, give, 0)
        pltpu.make_async_copy(y_out.at[half, rows8(seq)], y_in.at[half, here8], many.at[6 + half]).start()

    for half in range(2):
        pltpu.make_async_copy(gate_in.at[half], gate_in.at[half], many.at[3 + half]).wait()
        convolve(2 * half)
        convolve(2 * half + 1)
        give_y(half)

    own_outer.wait()
    arrived(-4, outer.at[:, theirs])
    for half in range(2):
        pltpu.make_async_copy(y_in.at[half], y_in.at[half], many.at[6 + half]).wait()
        for side in range(2):
            cols = slice(side * WIDTH + half * SIDE, side * WIDTH + (half + 1) * SIDE)
            for j in range(2):
                value = outer[j, cols, :] * y_in[half, pl.ds(side * WIDTH + j, SIDE, stride=2), :]
                out[j * SIDE : (j + 1) * SIDE, cols] = value.T

    for copy in started:
        copy.wait_send()
    for number, ref, rows in ((0, filt_t, 8), (2, gate_t, 16), (5, y_out, 8)):
        sent = ref.at[:, pl.ds(rows, 2 * WIDTH - rows)]
        pltpu.make_async_copy(sent, sent, many.at[number]).wait()


SLOTS = 112


def local(tokens, in_weight, short_filter, long_filter, skip_gain):
    width = skip_gain.shape[0]
    weights = in_weight.transpose(1, 0, 2)
    held = tables()
    vmem = pl.BlockSpec(memory_space=pltpu.VMEM)
    anywhere = pl.BlockSpec(memory_space=pl.ANY)
    out = pl.pallas_call(
        kernel,
        out_shape=jax.ShapeDtypeStruct((TOK, width), F32),
        in_specs=[anywhere] * (5 + len(held)),
        out_specs=vmem,
        scratch_shapes=[
            pltpu.VMEM((TOK, width), F32),
            pltpu.VMEM((TAPS, 3, width), F32),
            pltpu.SMEM((width,), F32),
            *[pltpu.VMEM(table.shape, table.dtype) for table in held],
            pltpu.VMEM((BLOCKS, 3, 2 * WROWS, WIDTH), BF16),
            pltpu.VMEM((HALO + POS, CH * FEAT), BF16),
            pltpu.VMEM((HALO + POS, COLS), F32),
            pltpu.VMEM((2, 2 * WIDTH, SIDE), F32),
            pltpu.VMEM((2, 2 * WIDTH, SIDE), F32),
            pltpu.VMEM((2, 2 * WIDTH, SIDE), F32),
            pltpu.VMEM((2, 2 * WIDTH, SIDE), F32),
            pltpu.VMEM((4, WIDTH, SIDE), F32),
            pltpu.VMEM((2, 2 * WIDTH, SIDE), F32),
            pltpu.VMEM((2, 2 * WIDTH, SIDE), F32),
            pltpu.VMEM((2, 2 * WIDTH, SIDE), F32),
            pltpu.VMEM((OWN * SIDE, 2 * SIDE), F32),
            pltpu.SemaphoreType.DMA((SLOTS,)),
            pltpu.SemaphoreType.DMA((SLOTS,)),
            pltpu.SemaphoreType.DMA((8,)),
        ],
        compiler_params=pltpu.CompilerParams(
            collective_id=0, has_side_effects=True, vmem_limit_bytes=60 * 1024 * 1024
        ),
    )(tokens, weights, long_filter, short_filter, skip_gain, *held)
    return out.astype(BF16)


def solution(mesh):
    placed = (P("seq", "ch"), P("seq", None, "ch"), P(None, None, "ch"), P("seq", "ch"), P("ch"))
    return jax.shard_map(
        local, mesh=mesh, in_specs=placed, out_specs=P("seq", "ch"), check_vma=False
    )
```

time: 117 us -> 94.6 us (0.81); the launches traced: 115 us -> 94.5 us
  Pallas kernels: 107 us -> 92.7 us
  local copies, waits for them, and re-layouts: 6.65 us -> 0 us
    pallas_call x1, Pallas kernels: 107 us -> 92.7 us  [local(): pl.pallas_call(kernel, out_shape=jax.ShapeDtypeStruct((TOK, width), F32),...]
    unnamed x16 -> x0, local copies, waits for them, and re-layouts: 4.46 us -> none
    reshape x4 -> x0, local copies, waits for them, and re-layouts: 2.19 us -> none  [the longest x3 1.43 us: local(): in_weight.reshape(WROWS, 3, 2, WIDTH).transpose(2, 0, 1, 3)]
where the time goes in v2:
time: 94.6 us; the launch traced here: 94.5 us
  Pallas kernels  92.7 us (98%)
  other arithmetic  1.78 us (2%)
    pallas_call x1, Pallas kernels, local(): pl.pallas_call(kernel, out_shape=jax.ShapeDtypeStruct((TOK, width), F32),...  92.7 us

profile of v2, /device:TPU:2, one launch (start us, length us, event | category | flops | bytes accessed | tf_op | source)
XLA Modules:
  0.0 94.5 jit_solution(17464279850581271238)
XLA Ops:
  0.0 92.7 %shard_map.100 = f32[256,512]{1,0:T(8,128)} custom-call(bf16[256,1024]{1,0:T(8,128)(2,1)} %tokens.1, bf16[3,64,512]{2,1,0:T(8,128)(2,1)} %bitcast.1, f32[256,512]{1,0:T(8,128)} %filt_hbm.1, f32[3,3,512]{2,1,0:T(4,128)} %taps_hbm.1, f32[512]{0:T(512)} %skip_hbm.1, bf16[256,384]{1,0:T(8,128)(2,1)} %constant.10.clone.first_hbm, ...), custom_call_target="tpu_custom_call" | custom-call | tf_op jit(solution)/shard_map/pallas_call | solution.py:473
  92.7 1.8 %convert_element_type.3 = bf16[256,512]{1,0:T(8,128)(2,1)} convert(f32[256,512]{1,0:T(8,128)} %shard_map.100) | non-fusion elementwise | flops 131072 | bytes 786432 | tf_op jit(solution)/shard_map/convert_element_type | solution.py:503

commit v3 on v2

--- a/solution.py
+++ b/solution.py
@@ -33,7 +33,7 @@
 REST = 2 * WROWS - SPLIT
 
 
-SWAP, ZF_OWN, ZF_ADDED, ZF, ZFY_OWN, ZFY_ADDED, ZFY, YF, PLANE, TOKEN, CORE, LAST_ROWS, TURN, GIVE, RESPOND, PROJECT = range(16)
+SWAP, ZF_OWN, ZF_ADDED, ZF, ZFY_OWN, ZFY_ADDED, ZFY, YF, PLANE, TOKEN, CORE, LAST_ROWS, GIVE, RESPOND, PROJECT = (*range(12), 13, 14, 15)
 
 
 def key(kind, first=0, second=0):
@@ -41,7 +41,7 @@
 
 
 STEPS = (
-    44, 454, 434, 134, 154, 1244, 1044, 954, 934, 1304, 1314, 534, 554, 254, 734, 754, 234, 1324, 642, 646, 655,
+    44, 454, 434, 134, 154, 1044, 954, 934, 1304, 1314, 534, 554, 254, 734, 754, 234, 1324, 642, 646, 655,
     653, 364, 633, 635, 324, 1334, 724, 764, 1344, 1354, 1054, 964, 856, 834, 835, 836, 857, 855, 837, 854, 1034,
     924, 1364, 665, 663, 625, 623, 314, 374, 652, 656, 632, 636, 1064, 1024, 1144, 866, 824, 825, 826, 867, 865,
     827, 864, 1444, 662, 626, 622, 666, 615, 613, 304, 675, 673, 384, 1544, 1554, 1534, 876, 814, 815, 877, 875,
@@ -120,6 +120,16 @@
     twin = {"ch": x_hi * 2 + 1 - core}
     mate = {"seq": seq_of(z, y, 1 - x_lo)}
 
+    barrier = pltpu.get_barrier_semaphore()
+
+    def greet(i, _):
+        pl.semaphore_signal(barrier, inc=1, device_id={"seq": (seq + i) % SEQ}, device_id_type=MESH)
+        return 0
+
+    lax.fori_loop(1, SEQ, greet, 0)
+    pl.semaphore_signal(barrier, inc=1, device_id=twin, device_id_type=MESH)
+    pl.semaphore_signal(barrier, inc=1, device_id=at_x(3 + 2 * x_lo), device_id_type=MESH)
+
     started = []
     slots = {}
 
@@ -181,18 +191,21 @@
         )
     ]
 
-    barrier = pltpu.get_barrier_semaphore()
-
-    def greet(i, _):
-        pl.semaphore_signal(barrier, inc=1, device_id={"seq": (seq + i) % SEQ}, device_id_type=MESH)
-        return 0
-
-    lax.fori_loop(1, SEQ, greet, 0)
-    pl.semaphore_signal(barrier, inc=1, device_id=twin, device_id_type=MESH)
-    pl.semaphore_signal(barrier, inc=1, device_id=at_x(3 + 2 * x_lo), device_id_type=MESH)
+    def rows8(index):
+        return pl.ds(pl.multiple_of(index * 8, 8), 8)
+
+    def rows16(index):
+        return pl.ds(pl.multiple_of(index * 16, 16), 16)
+
+    own_filt.wait()
+    for i in range(4):
+        for j in range(2):
+            filt_t[i % 2, pl.ds((i // 2) * WIDTH + j, SIDE, stride=2), :] = filt[
+                j * 128 : (j + 1) * 128, i * 128 : (i + 1) * 128
+            ].T
+    pltpu.make_async_copy(filt_t.at[:, rows8(x_lo * BLOCKS + blk)], filt_in.at[:, rows8(seq)], many.at[1]).start()
+    own_w.wait()
     pl.semaphore_wait(barrier, SEQ + 1)
-
-    own_w.wait()
 
     copies = {}
 
@@ -284,21 +297,6 @@
 
         lax.fori_loop(0, 3, part, 0)
 
-    def rows8(index):
-        return pl.ds(pl.multiple_of(index * 8, 8), 8)
-
-    def rows16(index):
-        return pl.ds(pl.multiple_of(index * 16, 16), 16)
-
-    def turn_filter():
-        own_filt.wait()
-        for i in range(4):
-            for j in range(2):
-                filt_t[i % 2, pl.ds((i // 2) * WIDTH + j, SIDE, stride=2), :] = filt[
-                    j * 128 : (j + 1) * 128, i * 128 : (i + 1) * 128
-                ].T
-        pltpu.make_async_copy(filt_t.at[:, rows8(x_lo * BLOCKS + blk)], filt_in.at[:, rows8(seq)], many.at[1]).start()
-
     def give_filter(part):
         def give(i, _):
             peer = (seq + SPREAD * i) % SEQ
@@ -359,8 +357,6 @@
             fresh = False
         elif kind == GIVE:
             give_filter(number + 4)
-        elif kind == TURN:
-            turn_filter()
         else:
             respond()
     assert here == set(copies)
@@ -382,7 +378,8 @@
         lax.fori_loop(1, BLOCKS, give, 0)
         pltpu.make_async_copy(gate_t.at[half, rows16(blk)], gate_in.at[half, rows16(blk)], many.at[3 + half]).start()
 
-    for half in range(2):
+    for stage in range(4):
+        half = stage % 2
         lanes = slice(half * SIDE, (half + 1) * SIDE)
         for row in range(4):
 
@@ -395,11 +392,22 @@
                     total = term if total is None else total + term
                 return total
 
-            gate_t[half, pl.ds(row, SIDE, stride=4), :] = (short(1) * short(2)).T
-            outer_t[row, lanes, :] = short(0).T
-        give_gate(half)
+            if stage < 2:
+                gate_t[half, pl.ds(row, SIDE, stride=4), :] = (short(1) * short(2)).T
+            else:
+                outer_t[row, lanes, :] = short(0).T
+        if stage < 2:
+            give_gate(half)
     go(-4, outer_t.at[pl.ds(2 * (1 - x_lo), 2)], outer.at[:, mine], mate)
     own_outer = local(-12, outer_t.at[pl.ds(2 * x_lo, 2)], outer.at[:, mine])
+
+    def all_sent(number, ref, rows):
+        sent = ref.at[:, pl.ds(rows, 2 * WIDTH - rows)]
+        pltpu.make_async_copy(sent, sent, many.at[number]).wait()
+
+    for copy in started[:-1]:
+        copy.wait_send()
+    all_sent(0, filt_t, 8)
 
     def convolve(pair):
         spectrum = transform(load_gate, pair)
@@ -444,6 +452,8 @@
         convolve(2 * half + 1)
         give_y(half)
 
+    started[-1].wait_send()
+    all_sent(2, gate_t, 16)
     own_outer.wait()
     arrived(-4, outer.at[:, theirs])
     for half in range(2):
@@ -454,11 +464,7 @@
                 value = outer[j, cols, :] * y_in[half, pl.ds(side * WIDTH + j, SIDE, stride=2), :]
                 out[j * SIDE : (j + 1) * SIDE, cols] = value.T
 
-    for copy in started:
-        copy.wait_send()
-    for number, ref, rows in ((0, filt_t, 8), (2, gate_t, 16), (5, y_out, 8)):
-        sent = ref.at[:, pl.ds(rows, 2 * WIDTH - rows)]
-        pltpu.make_async_copy(sent, sent, many.at[number]).wait()
+    all_sent(5, y_out, 8)
 
 
 SLOTS = 112

time: 94.6 us -> 94 us (level)
  no operation moved by 1% of the time
where the time goes in v3:
time: 94 us; the launch traced here: 93.9 us
  Pallas kernels  92.1 us (98%)
  other arithmetic  1.78 us (2%)
    pallas_call x1, Pallas kernels, local(): pl.pallas_call(kernel, out_shape=jax.ShapeDtypeStruct((TOK, width), F32),...  92.1 us

profile of v3, /device:TPU:2, one launch (start us, length us, event | category | flops | bytes accessed | tf_op | source)
XLA Modules:
  0.0 93.9 jit_solution(11392437043182998264)
XLA Ops:
  0.0 92.1 %shard_map.100 = f32[256,512]{1,0:T(8,128)} custom-call(bf16[256,1024]{1,0:T(8,128)(2,1)} %tokens.1, bf16[3,64,512]{2,1,0:T(8,128)(2,1)} %bitcast.1, f32[256,512]{1,0:T(8,128)} %filt_hbm.1, f32[3,3,512]{2,1,0:T(4,128)} %taps_hbm.1, f32[512]{0:T(512)} %skip_hbm.1, bf16[256,384]{1,0:T(8,128)(2,1)} %constant.10.clone.first_hbm, ...), custom_call_target="tpu_custom_call" | custom-call | tf_op jit(solution)/shard_map/pallas_call | solution.py:479
  92.1 1.8 %convert_element_type.3 = bf16[256,512]{1,0:T(8,128)(2,1)} convert(f32[256,512]{1,0:T(8,128)} %shard_map.100) | non-fusion elementwise | flops 131072 | bytes 786432 | tf_op jit(solution)/shard_map/convert_element_type | solution.py:509

commit v4 on v3

--- a/solution.py
+++ b/solution.py
@@ -29,6 +29,7 @@
 SIDE = 128
 LENGTH = SIDE * SIDE
 SPREAD = 27
+ROWS = 512
 LO, HI = pl.ds(0, WIDTH // 2), pl.ds(WIDTH // 2, WIDTH // 2)
 REST = 2 * WROWS - SPLIT
 
@@ -337,7 +338,8 @@
     def respond():
         for copy in tables_in:
             copy.wait()
-        pltpu.make_async_copy(filt_in, filt_in, many.at[1]).wait()
+        whole = filt_in.at[:, pl.ds(0, ROWS)]
+        pltpu.make_async_copy(whole, whole, many.at[1]).wait()
         for pair in range(OWN // 2):
             spec[pair * 256 : (pair + 1) * 256, :] = transform(load_filter, pair)
 
@@ -402,7 +404,7 @@
     own_outer = local(-12, outer_t.at[pl.ds(2 * x_lo, 2)], outer.at[:, mine])
 
     def all_sent(number, ref, rows):
-        sent = ref.at[:, pl.ds(rows, 2 * WIDTH - rows)]
+        sent = ref.at[:, pl.ds(rows, ROWS - rows)]
         pltpu.make_async_copy(sent, sent, many.at[number]).wait()
 
     for copy in started[:-1]:
@@ -447,7 +449,8 @@
         pltpu.make_async_copy(y_out.at[half, rows8(seq)], y_in.at[half, here8], many.at[6 + half]).start()
 
     for half in range(2):
-        pltpu.make_async_copy(gate_in.at[half], gate_in.at[half], many.at[3 + half]).wait()
+        whole = gate_in.at[half, pl.ds(0, ROWS)]
+        pltpu.make_async_copy(whole, whole, many.at[3 + half]).wait()
         convolve(2 * half)
         convolve(2 * half + 1)
         give_y(half)
@@ -457,7 +460,8 @@
     own_outer.wait()
     arrived(-4, outer.at[:, theirs])
     for half in range(2):
-        pltpu.make_async_copy(y_in.at[half], y_in.at[half], many.at[6 + half]).wait()
+        whole = y_in.at[half, pl.ds(0, ROWS)]
+        pltpu.make_async_copy(whole, whole, many.at[6 + half]).wait()
         for side in range(2):
             cols = slice(side * WIDTH + half * SIDE, side * WIDTH + (half + 1) * SIDE)
             for j in range(2):
@@ -489,14 +493,14 @@
             pltpu.VMEM((BLOCKS, 3, 2 * WROWS, WIDTH), BF16),
             pltpu.VMEM((HALO + POS, CH * FEAT), BF16),
             pltpu.VMEM((HALO + POS, COLS), F32),
-            pltpu.VMEM((2, 2 * WIDTH, SIDE), F32),
-            pltpu.VMEM((2, 2 * WIDTH, SIDE), F32),
-            pltpu.VMEM((2, 2 * WIDTH, SIDE), F32),
-            pltpu.VMEM((2, 2 * WIDTH, SIDE), F32),
+            pltpu.VMEM((2, ROWS + 16, SIDE), F32),
+            pltpu.VMEM((2, ROWS + 16, SIDE), F32),
+            pltpu.VMEM((2, ROWS + 16, SIDE), F32),
+            pltpu.VMEM((2, ROWS + 16, SIDE), F32),
             pltpu.VMEM((4, WIDTH, SIDE), F32),
             pltpu.VMEM((2, 2 * WIDTH, SIDE), F32),
-            pltpu.VMEM((2, 2 * WIDTH, SIDE), F32),
-            pltpu.VMEM((2, 2 * WIDTH, SIDE), F32),
+            pltpu.VMEM((2, ROWS + 16, SIDE), F32),
+            pltpu.VMEM((2, ROWS + 16, SIDE), F32),
             pltpu.VMEM((OWN * SIDE, 2 * SIDE), F32),
             pltpu.SemaphoreType.DMA((SLOTS,)),
             pltpu.SemaphoreType.DMA((SLOTS,)),

time: 94 us -> 94 us (level)
  no operation moved by 1% of the time
where the time goes in v4:
time: 94 us; the launch traced here: 93.9 us
  Pallas kernels  92.1 us (98%)
  other arithmetic  1.78 us (2%)
    pallas_call x1, Pallas kernels, local(): pl.pallas_call(kernel, out_shape=jax.ShapeDtypeStruct((TOK, width), F32),...  92.1 us

profile of v4, /device:TPU:2, one launch (start us, length us, event | category | flops | bytes accessed | tf_op | source)
XLA Modules:
  0.0 93.9 jit_solution(7594077692870876289)
XLA Ops:
  0.0 92.1 %shard_map.100 = f32[256,512]{1,0:T(8,128)} custom-call(bf16[256,1024]{1,0:T(8,128)(2,1)} %tokens.1, bf16[3,64,512]{2,1,0:T(8,128)(2,1)} %bitcast.1, f32[256,512]{1,0:T(8,128)} %filt_hbm.1, f32[3,3,512]{2,1,0:T(4,128)} %taps_hbm.1, f32[512]{0:T(512)} %skip_hbm.1, bf16[256,384]{1,0:T(8,128)(2,1)} %constant.10.clone.first_hbm, ...), custom_call_target="tpu_custom_call" | custom-call | tf_op jit(solution)/shard_map/pallas_call | solution.py:483
  92.1 1.8 %convert_element_type.3 = bf16[256,512]{1,0:T(8,128)(2,1)} convert(f32[256,512]{1,0:T(8,128)} %shard_map.100) | non-fusion elementwise | flops 131072 | bytes 786432 | tf_op jit(solution)/shard_map/convert_element_type | solution.py:513

commit v5 on v4

--- a/solution.py
+++ b/solution.py
@@ -380,8 +380,7 @@
         lax.fori_loop(1, BLOCKS, give, 0)
         pltpu.make_async_copy(gate_t.at[half, rows16(blk)], gate_in.at[half, rows16(blk)], many.at[3 + half]).start()
 
-    for stage in range(4):
-        half = stage % 2
+    for half, gated in ((0, True), (0, False), (1, False), (1, True)):
         lanes = slice(half * SIDE, (half + 1) * SIDE)
         for row in range(4):
 
@@ -394,11 +393,11 @@
                     total = term if total is None else total + term
                 return total
 
-            if stage < 2:
+            if gated:
                 gate_t[half, pl.ds(row, SIDE, stride=4), :] = (short(1) * short(2)).T
             else:
                 outer_t[row, lanes, :] = short(0).T
-        if stage < 2:
+        if gated:
             give_gate(half)
     go(-4, outer_t.at[pl.ds(2 * (1 - x_lo), 2)], outer.at[:, mine], mate)
     own_outer = local(-12, outer_t.at[pl.ds(2 * x_lo, 2)], outer.at[:, mine])
@@ -466,7 +465,7 @@
             cols = slice(side * WIDTH + half * SIDE, side * WIDTH + (half + 1) * SIDE)
             for j in range(2):
                 value = outer[j, cols, :] * y_in[half, pl.ds(side * WIDTH + j, SIDE, stride=2), :]
-                out[j * SIDE : (j + 1) * SIDE, cols] = value.T
+                out[j * SIDE : (j + 1) * SIDE, cols] = value.T.astype(BF16)
 
     all_sent(5, y_out, 8)
 
@@ -482,7 +481,7 @@
     anywhere = pl.BlockSpec(memory_space=pl.ANY)
     out = pl.pallas_call(
         kernel,
-        out_shape=jax.ShapeDtypeStruct((TOK, width), F32),
+        out_shape=jax.ShapeDtypeStruct((TOK, width), BF16),
         in_specs=[anywhere] * (5 + len(held)),
         out_specs=vmem,
         scratch_shapes=[
@@ -510,7 +509,7 @@
             collective_id=0, has_side_effects=True, vmem_limit_bytes=60 * 1024 * 1024
         ),
     )(tokens, weights, long_filter, short_filter, skip_gain, *held)
-    return out.astype(BF16)
+    return out
 
 
 def solution(mesh):

time: 94 us -> 93.8 us (level)
  other arithmetic: 1.78 us -> 0 us
  local copies, waits for them, and re-layouts: 0 us -> 1.67 us
    convert_element_type x1 -> x0, other arithmetic: 1.78 us -> none  [local(): return out.astype(BF16)]
    unnamed x0 -> x1, local copies, waits for them, and re-layouts: none -> 1.67 us
where the time goes in v5:
time: 93.8 us; the launch traced here: 93.6 us
  Pallas kernels  92 us (98%)
  local copies, waits for them, and re-layouts  1.67 us (2%)
    pallas_call x1, Pallas kernels, local(): pl.pallas_call(kernel, out_shape=jax.ShapeDtypeStruct((TOK, width), BF16)...  92 us

profile of v5, /device:TPU:2, one launch (start us, length us, event | category | flops | bytes accessed | tf_op | source)
XLA Modules:
  0.0 93.6 jit_solution(4461316740411059965)
XLA Ops:
  0.0 92.0 %shard_map.100 = bf16[256,512]{1,0:T(8,128)(2,1)} custom-call(bf16[256,1024]{1,0:T(8,128)(2,1)} %tokens.1, bf16[3,64,512]{2,1,0:T(8,128)(2,1)} %bitcast.1, f32[256,512]{1,0:T(8,128)} %filt_hbm.1, f32[3,3,512]{2,1,0:T(4,128)} %taps_hbm.1, f32[512]{0:T(512)} %skip_hbm.1, bf16[256,384]{1,0:T(8,128)(2,1)} %constant.10.clone.first_hbm, ...), custom_call_target="tpu_custom_call" | custom-call | tf_op jit(solution)/shard_map/pallas_call | solution.py:482
  92.0 1.7 %copy.12 = bf16[256,512]{1,0:T(8,128)(2,1)} copy(bf16[256,512]{1,0:T(8,128)(2,1)} %shard_map.100) | data formatting | bytes 524288

commit v6 on v4

--- a/solution.py
+++ b/solution.py
@@ -44,9 +44,9 @@
 STEPS = (
     44, 454, 434, 134, 154, 1044, 954, 934, 1304, 1314, 534, 554, 254, 734, 754, 234, 1324, 642, 646, 655,
     653, 364, 633, 635, 324, 1334, 724, 764, 1344, 1354, 1054, 964, 856, 834, 835, 836, 857, 855, 837, 854, 1034,
-    924, 1364, 665, 663, 625, 623, 314, 374, 652, 656, 632, 636, 1064, 1024, 1144, 866, 824, 825, 826, 867, 865,
+    924, 1364, 665, 663, 625, 623, 314, 374, 656, 632, 652, 636, 1064, 1024, 1144, 866, 824, 825, 826, 867, 865,
     827, 864, 1444, 662, 626, 622, 666, 615, 613, 304, 675, 673, 384, 1544, 1554, 1534, 876, 814, 815, 877, 875,
-    817, 874, 816, 1564, 685, 683, 1524, 612, 672, 616, 676, 886, 804, 805, 887, 885, 884, 806, 807, 682, 686, 1514,
+    1564, 817, 874, 816, 685, 683, 1524, 612, 672, 616, 676, 886, 804, 805, 887, 885, 884, 806, 807, 682, 686, 1514,
     1574, 1584,
 )
 

time: 94 us -> 94 us (level)
  no operation moved by 1% of the time
where the time goes in v6:
time: 94 us; the launch traced here: 93.9 us
  Pallas kernels  92.1 us (98%)
  other arithmetic  1.78 us (2%)
    pallas_call x1, Pallas kernels, local(): pl.pallas_call(kernel, out_shape=jax.ShapeDtypeStruct((TOK, width), F32),...  92.1 us

profile of v6, /device:TPU:2, one launch (start us, length us, event | category | flops | bytes accessed | tf_op | source)
XLA Modules:
  0.0 93.9 jit_solution(16529003587630918878)
XLA Ops:
  0.0 92.1 %shard_map.100 = f32[256,512]{1,0:T(8,128)} custom-call(bf16[256,1024]{1,0:T(8,128)(2,1)} %tokens.1, bf16[3,64,512]{2,1,0:T(8,128)(2,1)} %bitcast.1, f32[256,512]{1,0:T(8,128)} %filt_hbm.1, f32[3,3,512]{2,1,0:T(4,128)} %taps_hbm.1, f32[512]{0:T(512)} %skip_hbm.1, bf16[256,384]{1,0:T(8,128)(2,1)} %constant.10.clone.first_hbm, ...), custom_call_target="tpu_custom_call" | custom-call | tf_op jit(solution)/shard_map/pallas_call | solution.py:483
  92.1 1.8 %convert_element_type.3 = bf16[256,512]{1,0:T(8,128)(2,1)} convert(f32[256,512]{1,0:T(8,128)} %shard_map.100) | non-fusion elementwise | flops 131072 | bytes 786432 | tf_op jit(solution)/shard_map/convert_element_type | solution.py:513
